TPU v7x, 32 devices: a whole 2x2x4 slice. The times are simulated.
32 devices in a mesh: group: 2 (over y), ctx: 8 (over z, x), tp: 2 (over core).
Axes of the slice: x: 2, y: 2, z: 4, core: 2. Of those that a mesh axis runs over, the one named last changes fastest.
Arguments:
- hidden: bfloat16 [256, 16384], P(('group', 'ctx')), parts along dimension 0, may hold values from -6 to 6
- q_base: bfloat16 [256, 8192], P(('group', 'ctx'), 'tp'), parts along dimension 0, may hold values from -6 to 6
- adapter_down: bfloat16 [16, 16384, 64], P(('group', 'ctx')), parts along dimension 0, may hold values from -0.046875 to 0.046875
- adapter_up: bfloat16 [16, 64, 8192], P(('group', 'ctx'), None, 'tp'), parts along dimension 0, may hold values from -0.75 to 0.75
- adapter_owner: int32 [2], P('group'), parts along dimension 0, may hold values from 0 to 7
- turn_start: int32 [2], P('group'), parts along dimension 0, may hold values from 512 to 2047
- shard_lengths: int32 [16], P('group'), parts along dimension 0, may hold values from 1 to 64, 384 in all
- stored_keys: bfloat16 [1024, 512], P(('group', 'ctx'), 'tp'), parts along dimension 0, may hold values from -250 to 250
- stored_values: bfloat16 [1024, 512], P(('group', 'ctx'), 'tp'), parts along dimension 0, may hold values from -6 to 6
- unrotated_turn_keys: bfloat16 [256, 512], P(('group', 'ctx'), 'tp'), parts along dimension 0, may hold values from -15 to 15
- incoming_values: bfloat16 [256, 512], P(('group', 'ctx'), 'tp'), parts along dimension 0, may hold values from -6 to 6
Outputs:
- attended: bfloat16 [256, 8192], P(('group', 'ctx'), 'tp'), parts along dimension 0
There are 2 independent parts, one for each index of `group`. A program takes and returns all parts, laid end to end along the dimension named above; each array names one. Nothing has to cross between parts.
Inputs may be any that keep to these rules, and one draw needn't show every extreme that they name: The used slots of shard s are its slots 0 .. shard_lengths[s] - 1; some shard uses all 64.
All inputs are finite; a program needn't handle non-finite values.
Results may differ from a plain program's by a relative error of at most 0.019.
The roundings to bfloat16 on the way count: a program that leaves them out, or rounds other values in their place, can miss the bound.
Values may be sent and summed in bfloat16 or wider, within the bound.
A program may use at most 64 MiB of HBM per device.

v0:
```python
import math

import jax
import jax.numpy as jnp
from jax import lax
from jax.sharding import PartitionSpec as P

HEAD_SIZE = 128


def spread(shard, axis, root):
    mine = lax.axis_index(axis) == root
    return lax.psum(jnp.where(mine, shard, jnp.zeros_like(shard)), axis)


def apply_rotary(values, token_positions, heads):
    half_dim = HEAD_SIZE // 2
    inverse = jnp.exp(
        jnp.arange(half_dim, dtype=jnp.float32) * (-2.0 * math.log(500000.0) / HEAD_SIZE)
    )
    angles = token_positions.astype(jnp.float32)[:, None] * inverse[None, :]
    cosine = jnp.cos(angles)[:, None, :]
    sine = jnp.sin(angles)[:, None, :]
    shaped = values.reshape(values.shape[0], heads, HEAD_SIZE)
    first = shaped[..., :half_dim]
    second = shaped[..., half_dim:]
    turned = jnp.concatenate(
        [first * cosine - second * sine, second * cosine + first * sine], axis=-1
    )
    return turned.reshape(values.shape[0], heads * HEAD_SIZE)


def shards(
    hidden,
    q_base,
    adapter_down,
    adapter_up,
    adapter_owner,
    turn_start,
    shard_lengths,
    stored_keys,
    stored_values,
    unrotated_turn_keys,
    incoming_values,
):
    holder = adapter_owner[0]
    slot_down = adapter_down[0]
    slot_up = adapter_up[0]
    got_down, got_up = (spread(slot_down, "ctx", holder), spread(slot_up, "ctx", holder))
    lowrank = jnp.dot(hidden, got_down, preferred_element_type=jnp.float32).astype(jnp.bfloat16)
    adapter_delta = jnp.dot(lowrank, got_up, preferred_element_type=jnp.float32)
    token_count = q_base.shape[0]
    slot_count = stored_keys.shape[0]
    shard_rows = token_count + slot_count
    ctx_size = lax.axis_size("ctx")
    myself = lax.axis_index("ctx")
    query_heads = q_base.shape[1] // HEAD_SIZE
    kv_heads = unrotated_turn_keys.shape[1] // HEAD_SIZE
    groups = query_heads // kv_heads
    local_tokens = jnp.arange(token_count, dtype=jnp.int32)
    token_positions = turn_start[0] + myself * token_count + local_tokens
    query_rows = apply_rotary(
        q_base.astype(jnp.float32) + 0.5 * adapter_delta, token_positions, query_heads
    ).astype(jnp.bfloat16)
    rotated_turn_keys = apply_rotary(
        unrotated_turn_keys.astype(jnp.float32), token_positions, kv_heads
    ).astype(jnp.bfloat16)
    grouped = query_rows.reshape(token_count, kv_heads, groups, HEAD_SIZE)
    key_here = jnp.concatenate([stored_keys, rotated_turn_keys], axis=0)
    value_here = jnp.concatenate([stored_values, incoming_values], axis=0)
    mine = myself * token_count + local_tokens
    score_scale = 1.0 / math.sqrt(HEAD_SIZE)
    shard_ids = jnp.arange(ctx_size, dtype=jnp.int32)

    def absorb(state, key_block, value_block, start):
        highest, denominator, accum = state
        row_count = key_block.shape[0]
        global_rows = start + jnp.arange(row_count, dtype=jnp.int32)
        owner_shard = global_rows // shard_rows
        within = global_rows % shard_rows
        is_cache = within < slot_count
        lengths_here = jnp.sum(
            jnp.where(owner_shard[:, None] == shard_ids[None, :], shard_lengths[None, :], 0), axis=1
        )
        token_number = owner_shard * token_count + (within - slot_count)
        allowed = jnp.where(
            is_cache[None, :],
            (within < lengths_here)[None, :],
            token_number[None, :] <= mine[:, None],
        )
        allowed = allowed[:, None, None, :]
        key_head_rows = key_block.reshape(-1, kv_heads, HEAD_SIZE)
        value_head_rows = value_block.reshape(-1, kv_heads, HEAD_SIZE)
        scores = (
            jnp.einsum("rhgd,khd->rhgk", grouped, key_head_rows, preferred_element_type=jnp.float32)
            * score_scale
        )
        new_high = jnp.maximum(highest, jnp.max(jnp.where(allowed, scores, -1e30), axis=-1))
        weights = jnp.where(allowed, jnp.exp(scores - new_high[..., None]), 0.0)
        fade = jnp.exp(highest - new_high)
        denominator = denominator * fade + jnp.sum(weights, axis=-1)
        product = jnp.einsum(
            "rhgk,khd->rhgd",
            weights.astype(jnp.bfloat16),
            value_head_rows,
            preferred_element_type=jnp.float32,
        )
        accum = accum * fade[..., None] + product
        return (new_high, denominator, accum)

    initial = (
        jnp.full((token_count, kv_heads, groups), -1e30, jnp.float32),
        jnp.zeros((token_count, kv_heads, groups), jnp.float32),
        jnp.zeros((token_count, kv_heads, groups, HEAD_SIZE), jnp.float32),
    )
    block_rows = shard_rows * 8

    def fold_pieces(state, pieces, start):
        key_piece, value_piece = pieces
        row_count = key_piece.shape[0]
        if row_count > block_rows and row_count % block_rows == 0:
            count = row_count // block_rows
            key_split = key_piece.reshape(count, block_rows, key_piece.shape[1])
            value_split = value_piece.reshape(count, block_rows, value_piece.shape[1])

            def inner(carry, items):
                key_one, value_one, number = items
                return (absorb(carry, key_one, value_one, start + number * block_rows), None)

            numbers = jnp.arange(count, dtype=jnp.int32)
            state, unused = lax.scan(inner, state, (key_split, value_split, numbers))
            return state
        return absorb(state, key_piece, value_piece, start)

    state = fold_pieces(
        initial,
        (
            lax.all_gather(key_here, "ctx", axis=0, tiled=True),
            lax.all_gather(value_here, "ctx", axis=0, tiled=True),
        ),
        jnp.int32(0),
    )
    highest, denominator, accum = state
    attended = accum / denominator[..., None]
    return attended.reshape(token_count, query_heads * HEAD_SIZE).astype(jnp.bfloat16)


def solution(mesh):
    return jax.shard_map(
        shards,
        mesh=mesh,
        in_specs=(
            P(("group", "ctx"), None),
            P(("group", "ctx"), "tp"),
            P(("group", "ctx"), None, None),
            P(("group", "ctx"), None, "tp"),
            P("group"),
            P("group"),
            P("group"),
            P(("group", "ctx"), "tp"),
            P(("group", "ctx"), "tp"),
            P(("group", "ctx"), "tp"),
            P(("group", "ctx"), "tp"),
        ),
        out_specs=P(("group", "ctx"), "tp"),
        check_vma=False,
    )
```

profile of v0, /device:TPU:0, one launch (start us, length us, event | category | flops | bytes accessed | tf_op | source)
XLA Modules:
  0.0 146.1 jit_solution(9558791827877660342)
XLA Ops:
  6.5 0.0 copy-start
  6.5 0.0 all-reduce.3.cloned.1.call-start
  7.3 0.0 copy-start.1
  7.3 1.5 select_bitcast_fusion
  8.7 0.0 copy-done.1
  8.7 0.8 select_bitcast_fusion.1
  9.6 0.0 copy-start.5
  9.6 0.0 copy-start.3
  9.6 0.0 copy-start.4
  9.6 0.0 copy-start.6
  9.6 0.0 all-reduce.3.cloned.1.call-update
  9.6 0.0 copy-start.7
  9.6 0.0 copy-start.2
  10.3 0.0 copy-done.5
  10.4 0.1 multiply_cosine_fusion
  10.5 0.1 subtract_convert_fusion.1
  10.6 0.1 pad_maximum_fusion.3
  10.7 0.0 copy-done.3
  10.7 34.5 %all_gather.6 = bf16[640,256]{1,0:T(8,128)(2,1)S(1)} all-gather(bf16[80,256]{1,0:T(8,128)(2,1)S(1)} %pad_maximum_fusion.1), channel_id=1, replica_groups=mesh['group'=2,'ctx'=8,'tp'=2] {'ctx'}, dimensions={0}, use_global_device_ids=true | all-gather | bytes 368640 | tf_op jit(solution)/shard_map/all_gather | solution.py:138
  45.2 0.2 copy.39
  45.4 0.0 copy-done.4
  45.4 0.0 copy-done.6
  45.4 31.5 %all_gather.7 = bf16[640,256]{1,0:T(8,128)(2,1)S(1)} all-gather(bf16[80,256]{1,0:T(8,128)(2,1)S(1)} %pad_maximum_fusion.2), channel_id=1, replica_groups=mesh['group'=2,'ctx'=8,'tp'=2] {'ctx'}, dimensions={0}, use_global_device_ids=true | all-gather | bytes 368640 | tf_op jit(solution)/shard_map/all_gather | solution.py:139
  77.0 0.2 copy.42
  77.2 0.0 copy-done.7
  77.2 0.1 select_reduce_fusion.1
  77.3 0.1 compare_select_fusion
  77.4 56.8 %all-reduce.3.cloned.1.call-done = (bf16[64,4096]{1,0:T(8,128)(2,1)}, bf16[16384,64]{0,1:T(8,128)(2,1)}) async-done(((bf16[64,4096]{1,0:T(8,128)(2,1)}, bf16[16384,64]{0,1:T(8,128)(2,1)}), (bf16[64,4096]{1,0:T(8,128)(2,1)}, bf16[16384,64]{0,1:T(8,128)(2,1)})) %all-reduce.3.cloned.1.call-update) | async-done | bytes 2621456 | tf_op jit(solution)/shard_map/psum | solution.py:13
  134.2 0.0 copy-done
  134.2 0.0 copy-done.2
  134.2 2.6 %fusion.2 = f32[2,8,32,128]{3,1,2,0:T(8,128)S(1)} fusion(bf16[64,4096]{1,0:T(8,128)(2,1)} %get-tuple-element.5, bf16[16384,64]{0,1:T(8,128)(2,1)} %get-tuple-element.6, bf16[16,16384]{1,0:T(8,128)(2,1)S(1)} %copy-done, bf16[16,4096]{1,0:T(8,128)(2,1)S(1)} %copy-done.2), kind=kOutput, calls=%fused_computation.7 | convolution fusion | flops 42140672 | bytes 3538944 | tf_op jit(solution)/shard_map/dot_general | solution.py:51
  136.8 0.1 copy.52
  136.9 0.1 subtract_convert_fusion
  137.1 0.1 pad_maximum_fusion
  137.2 0.4 select_reduce_fusion
  137.6 0.4 fusion.6
  138.1 0.4 fusion.5
  138.5 0.7 copy.60
  (13 shorter events, 0.1 us)
Async XLA Ops:
  6.5 127.7 %copy-start = (bf16[16,16384]{1,0:T(8,128)(2,1)S(1)}, bf16[16,16384]{1,0:T(8,128)(2,1)}, u32[]{:S(2)}) copy-start(bf16[16,16384]{1,0:T(8,128)(2,1)} %param.11) | copy-start | bytes 1572868
  6.5 127.7 %all-reduce.3.cloned.1.call-start = ((), (), s32[]{:S(2)}) async-start(), calls=%async_computation | async-start | bytes 5242880 | tf_op jit(solution)/shard_map/psum | solution.py:13
  7.3 1.5 %copy-start.1 = (bf16[1,64,4096]{2,1,0:T(8,128)(2,1)S(1)}, bf16[1,64,4096]{2,1,0:T(8,128)(2,1)}, u32[]{:S(2)}) copy-start(bf16[1,64,4096]{2,1,0:T(8,128)(2,1)} %param.14) | copy-start | bytes 1572868
  9.6 0.8 copy-start.5
  9.6 1.1 copy-start.3
  9.6 35.9 %copy-start.4 = (bf16[64,256]{1,0:T(8,128)(2,1)S(1)}, bf16[64,256]{1,0:T(8,128)(2,1)}, u32[]{:S(2)}) copy-start(bf16[64,256]{1,0:T(8,128)(2,1)} %param.19) | copy-start | bytes 98308
  9.6 35.9 %copy-start.6 = (bf16[16,256]{1,0:T(8,128)(2,1)S(1)}, bf16[16,256]{1,0:T(8,128)(2,1)}, u32[]{:S(2)}) copy-start(bf16[16,256]{1,0:T(8,128)(2,1)} %param.21) | copy-start | bytes 24580
  9.6 67.6 %copy-start.7 = (s32[8]{0:T(128)S(1)}, s32[8]{0:T(128)}, u32[]{:S(2)}) copy-start(s32[8]{0:T(128)} %param.17) | copy-start | bytes 100
  9.6 124.6 %copy-start.2 = (bf16[16,4096]{1,0:T(8,128)(2,1)S(1)}, bf16[16,4096]{1,0:T(8,128)(2,1)}, u32[]{:S(2)}) copy-start(bf16[16,4096]{1,0:T(8,128)(2,1)} %param.12) | copy-start | bytes 393220
Sparse Core Ops, SparseCore 0:
  11.2 122.9 all-reduce.2
where the time goes:
time: 146 us
  blocking collectives  66 us (45%)
  waiting for transfers between devices  56.8 us (39%)
  between operations  15 us (10%)
  matrix products  3.5 us (2%)
  other arithmetic  3.49 us (2%)
    psum x1, waiting for transfers between devices, spread(): return lax.psum(jnp.where(mine, shard, jnp.zeros_like(shard)), axis)  56.8 us
    all_gather x1, blocking collectives, shards(): lax.all_gather(key_here, 'ctx', axis=0, tiled=True)  34.5 us
    all_gather x1, blocking collectives, shards(): lax.all_gather(value_here, 'ctx', axis=0, tiled=True)  31.5 us
  transfers between devices with their start and end apart: 1, of which 1 were waited for; matrix products, arithmetic and copies ran while one was open for 1% of the time, Pallas kernels for 0%

commit v1 on v0

--- a/solution.py
+++ b/solution.py
@@ -1,8 +1,11 @@
+import functools
 import math
 
 import jax
 import jax.numpy as jnp
 from jax import lax
+from jax.experimental import pallas as pl
+from jax.experimental.pallas import tpu as pltpu
 from jax.sharding import PartitionSpec as P
 
 HEAD_SIZE = 128
@@ -145,9 +148,344 @@
     return attended.reshape(token_count, query_heads * HEAD_SIZE).astype(jnp.bfloat16)
 
 
+MESH = pl.DeviceIdType.MESH
+
+
+def turn_kernel(
+    ctx_size, tp_size,
+    owner_ref, lengths_ref, cosine_ref, sine_ref,
+    hidden_ref, q_ref, down_ref, up_ref, keys_ref, values_ref, turn_keys_ref, turn_values_ref,
+    out_ref,
+    down_mine, down_pair, down_merged, down_cand,
+    up_mine, up_pair, up_merged, up_cand,
+    hid, base, cached_k, cached_v, fresh_k, fresh_v,
+    partial, partials, low_mine, low_all, attended,
+    pair_send, pair_recv, up_pair_send, up_pair_recv,
+    column_send, column_recv, rows_send, rows_recv, part_send, part_recv,
+    late_send, late_recv, local_sem,
+):
+    me = lax.axis_index("ctx")
+    core = lax.axis_index("tp")
+    column = lax.rem(me, 2)
+    row = me // 2
+    rows = ctx_size // 2
+    slot = column * rows + row
+    partner = me + 1 - 2 * column
+    tokens = hidden_ref.shape[0]
+    half = hidden_ref.shape[1] // tp_size
+    chunk = half // ctx_size
+    width = q_ref.shape[1] // ctx_size
+    slots = keys_ref.shape[0]
+    rank = down_ref.shape[0]
+
+    barrier = pltpu.get_barrier_semaphore()
+    for far in range(1, ctx_size * tp_size):
+        other = lax.rem(me + far // tp_size, ctx_size)
+        other_core = lax.rem(core + far % tp_size, tp_size)
+        pl.semaphore_signal(
+            barrier, inc=1, device_id={"ctx": other, "tp": other_core}, device_id_type=MESH
+        )
+
+    def slot_of(index):
+        return lax.rem(index, 2) * rows + index // 2
+
+    def features(number):
+        return pl.ds(pl.multiple_of(core * half + number * chunk, chunk), chunk)
+
+    def columns(number):
+        return pl.ds(pl.multiple_of(number * width, width), width)
+
+    def kv_columns(index):
+        return pl.ds(pl.multiple_of(lax.rem(index, 2) * HEAD_SIZE, HEAD_SIZE), HEAD_SIZE)
+
+    def block(index, size):
+        return pl.ds(pl.multiple_of(index * size, size), size)
+
+    local = []
+    for far in range(rows):
+        at = lax.rem(row + 1 + far, rows)
+        local.append((down_ref.at[:, features(column * rows + at)], down_mine.at[at]))
+        local.append((up_ref.at[:, columns(column * rows + at)], up_mine.at[at]))
+    local.append((hidden_ref.at[:, features(slot)], hid.at[block(me, tokens)]))
+    local.append((q_ref.at[:, columns(slot)], base.at[block(me, tokens)]))
+    local.append((keys_ref.at[:, kv_columns(me)], cached_k.at[block(me, slots)]))
+    local.append((values_ref.at[:, kv_columns(me)], cached_v.at[block(me, slots)]))
+    local.append((turn_keys_ref.at[:, kv_columns(me)], fresh_k.at[block(me, tokens)]))
+    local.append((turn_values_ref.at[:, kv_columns(me)], fresh_v.at[block(me, tokens)]))
+    local = [
+        pltpu.make_async_copy(source, target, local_sem.at[number])
+        for number, (source, target) in enumerate(local)
+    ]
+    for copy in local:
+        copy.start()
+
+    pl.semaphore_wait(barrier, ctx_size * tp_size - 1)
+
+    def remote(source, target, send, recv, index, to_core=None):
+        return pltpu.make_async_remote_copy(
+            src_ref=source, dst_ref=target, send_sem=send, recv_sem=recv,
+            device_id={"ctx": index, "tp": core if to_core is None else to_core},
+            device_id_type=MESH,
+        )
+
+    pair, up_copies = [], []
+    for far in range(rows):
+        at = lax.rem(row + 1 + far, rows)
+        pair.append(remote(
+            down_ref.at[:, features((1 - column) * rows + at)], down_pair.at[at],
+            pair_send.at[far], pair_recv.at[far], partner,
+        ))
+        up_copies.append(remote(
+            up_ref.at[:, columns((1 - column) * rows + at)], up_pair.at[at],
+            up_pair_send.at[far], up_pair_recv.at[far], partner,
+        ))
+    for copy in pair:
+        copy.start()
+
+    moved = []
+    for far in range(1, ctx_size):
+        to = lax.rem(me + far, ctx_size)
+        moved.append([
+            remote(source, target, rows_send.at[kind, far], rows_recv.at[kind, far], to)
+            for kind, (source, target) in enumerate([
+                (hidden_ref.at[:, features(slot_of(to))], hid.at[block(me, tokens)]),
+                (q_ref.at[:, columns(slot_of(to))], base.at[block(me, tokens)]),
+                (keys_ref.at[:, kv_columns(to)], cached_k.at[block(me, slots)]),
+                (values_ref.at[:, kv_columns(to)], cached_v.at[block(me, slots)]),
+                (turn_keys_ref.at[:, kv_columns(to)], fresh_k.at[block(me, tokens)]),
+                (turn_values_ref.at[:, kv_columns(to)], fresh_v.at[block(me, tokens)]),
+            ])
+        ])
+    for copies in moved:
+        copies[0].start()
+    for copy in up_copies:
+        copy.start()
+    for kind in range(1, 6):
+        for copies in moved:
+            copies[kind].start()
+
+    for copy in local:
+        copy.wait()
+
+    owner = owner_ref[0]
+    owner_row = owner // 2
+    is_mine = owner == me
+
+    def merge(copies, mine, other, merged, cand, kind):
+        sent = []
+        for far in range(rows):
+            at = lax.rem(row + 1 + far, rows)
+            copies[far].wait_recv()
+            chosen = lax.select_n(is_mine, other[at], mine[at])
+            if far == rows - 1:
+                cand[row] = chosen
+            else:
+                merged[at] = chosen
+                copy = remote(
+                    merged.at[at], cand.at[row],
+                    column_send.at[kind, far], column_recv.at[kind, far], at * 2 + column,
+                )
+                copy.start()
+                sent.append(copy)
+        return sent
+
+    down_sent = merge(pair, down_mine, down_pair, down_merged, down_cand, 0)
+    up_sent = merge(up_copies, up_mine, up_pair, up_merged, up_cand, 1)
+    for copies in moved:
+        copies[0].wait_recv()
+    for copy in down_sent:
+        copy.wait_recv()
+
+    product = lax.dot_general(
+        hid[...], down_cand[owner_row], (((1,), (1,)), ((), ())),
+        preferred_element_type=jnp.float32,
+    )
+    partial[...] = jnp.concatenate([product, jnp.zeros_like(product)], axis=1)
+    summed = []
+    mine_at = me * tp_size + core
+    for far in range(1, ctx_size * tp_size):
+        to = lax.rem(me + far // tp_size, ctx_size)
+        copy = remote(
+            partial.at[block(to, tokens)], partials.at[mine_at],
+            part_send.at[far], part_recv.at[far], to,
+            lax.rem(core + far % tp_size, tp_size),
+        )
+        copy.start()
+        summed.append(copy)
+    partials[mine_at] = partial[block(me, tokens)]
+    for copy in summed:
+        copy.wait_recv()
+    total = partials[0]
+    for number in range(1, ctx_size * tp_size):
+        total = total + partials[number]
+    lowrank = total.astype(jnp.bfloat16)
+    low_mine[...] = lowrank
+    low_all[block(me, tokens)] = lowrank
+    low_sent = []
+    for far in range(1, ctx_size):
+        copy = remote(
+            low_mine, low_all.at[block(me, tokens)],
+            late_send.at[0, far], late_recv.at[0, far], lax.rem(me + far, ctx_size),
+        )
+        copy.start()
+        low_sent.append(copy)
+
+    for kind in range(1, 6):
+        for copies in moved:
+            copies[kind].wait_recv()
+    for copy in up_sent:
+        copy.wait_recv()
+    cosine = cosine_ref[...]
+    sine = sine_ref[...]
+
+    def rotate(values):
+        return values * cosine + pltpu.roll(values, HEAD_SIZE // 2, 1) * sine
+
+    new_keys = rotate(fresh_k[...].astype(jnp.float32)).astype(jnp.bfloat16)
+    new_values = fresh_v[...]
+    old_keys = cached_k[...]
+    old_values = cached_v[...]
+    turn = tokens * ctx_size
+    cache = slots * ctx_size
+    place = lax.broadcasted_iota(jnp.int32, (turn, cache), 1)
+    used = place < lengths_ref[0]
+    for shard in range(1, ctx_size):
+        begin = shard * slots
+        used = used | ((place >= begin) & (place < begin + lengths_ref[shard]))
+    token = lax.broadcasted_iota(jnp.int32, (turn, turn), 0)
+    seen = lax.broadcasted_iota(jnp.int32, (turn, turn), 1) <= token
+    scale = 1.0 / math.sqrt(HEAD_SIZE)
+
+    for copy in low_sent:
+        copy.wait_recv()
+    delta = jnp.dot(
+        low_all[:, :rank], up_cand[owner_row], preferred_element_type=jnp.float32
+    )
+    contract = (((1,), (1,)), ((), ()))
+    for head in range(width // HEAD_SIZE):
+        lanes = slice(head * HEAD_SIZE, (head + 1) * HEAD_SIZE)
+        query = rotate(
+            base[:, lanes].astype(jnp.float32) + 0.5 * delta[:, lanes]
+        ).astype(jnp.bfloat16)
+        old = lax.dot_general(query, old_keys, contract, preferred_element_type=jnp.float32)
+        new = lax.dot_general(query, new_keys, contract, preferred_element_type=jnp.float32)
+        old = jnp.where(used, old * scale, -1e30)
+        new = jnp.where(seen, new * scale, -1e30)
+        top = jnp.maximum(
+            jnp.max(old, axis=1, keepdims=True), jnp.max(new, axis=1, keepdims=True)
+        )
+        old = jnp.where(used, jnp.exp(old - top), 0.0)
+        new = jnp.where(seen, jnp.exp(new - top), 0.0)
+        denominator = jnp.sum(old, axis=1, keepdims=True) + jnp.sum(new, axis=1, keepdims=True)
+        gathered = jnp.dot(
+            old.astype(jnp.bfloat16), old_values, preferred_element_type=jnp.float32
+        ) + jnp.dot(new.astype(jnp.bfloat16), new_values, preferred_element_type=jnp.float32)
+        attended[:, lanes] = (gathered / denominator).astype(jnp.bfloat16)
+
+    sent = []
+    for far in range(1, ctx_size):
+        to = lax.rem(me + far, ctx_size)
+        copy = remote(
+            attended.at[block(to, tokens)], out_ref.at[:, columns(slot)],
+            late_send.at[1, far], late_recv.at[1, far], to,
+        )
+        copy.start()
+        sent.append(copy)
+    out_ref[:, columns(slot)] = attended[block(me, tokens)]
+    for copy in sent:
+        copy.wait_recv()
+    for copies in [pair, up_copies, down_sent, up_sent, summed, low_sent, sent] + moved:
+        for copy in copies:
+            copy.wait_send()
+
+
+def turn_call(ctx_size, tp_size, *operands):
+    (
+        hidden, q_base, adapter_down, adapter_up, adapter_owner, turn_start, shard_lengths,
+        stored_keys, stored_values, unrotated_turn_keys, incoming_values,
+    ) = operands
+    tokens, features = hidden.shape
+    rank = adapter_down.shape[2]
+    slots = stored_keys.shape[0]
+    rows = ctx_size // 2
+    chunk = features // tp_size // ctx_size
+    width = q_base.shape[1] // ctx_size
+    turn = tokens * ctx_size
+    devices = ctx_size * tp_size
+    half_dim = HEAD_SIZE // 2
+    inverse = jnp.exp(
+        jnp.arange(half_dim, dtype=jnp.float32) * (-2.0 * math.log(500000.0) / HEAD_SIZE)
+    )
+    positions = turn_start[0] + jnp.arange(turn, dtype=jnp.int32)
+    angles = positions.astype(jnp.float32)[:, None] * inverse[None, :]
+    cosine, sine = jnp.cos(angles), jnp.sin(angles)
+    cosine = jnp.concatenate([cosine, cosine], axis=1)
+    sine = jnp.concatenate([-sine, sine], axis=1)
+    bf16, f32 = jnp.bfloat16, jnp.float32
+    vmem, smem = pl.BlockSpec(memory_space=pltpu.VMEM), pl.BlockSpec(memory_space=pltpu.SMEM)
+    anywhere = pl.BlockSpec(memory_space=pl.ANY)
+    dma = pltpu.SemaphoreType.DMA
+    return pl.pallas_call(
+        functools.partial(turn_kernel, ctx_size, tp_size),
+        out_shape=jax.ShapeDtypeStruct(q_base.shape, bf16),
+        in_specs=[smem, smem, vmem, vmem] + [anywhere] * 8,
+        out_specs=vmem,
+        scratch_shapes=[pltpu.VMEM((rows, rank, chunk), bf16)] * 4
+        + [pltpu.VMEM((rows, rank, width), bf16)] * 4
+        + [
+            pltpu.VMEM((turn, chunk), bf16),
+            pltpu.VMEM((turn, width), bf16),
+            pltpu.VMEM((slots * ctx_size, HEAD_SIZE), bf16),
+            pltpu.VMEM((slots * ctx_size, HEAD_SIZE), bf16),
+            pltpu.VMEM((turn, HEAD_SIZE), bf16),
+            pltpu.VMEM((turn, HEAD_SIZE), bf16),
+            pltpu.VMEM((turn, 2 * rank), f32),
+            pltpu.VMEM((devices, tokens, 2 * rank), f32),
+            pltpu.VMEM((tokens, 2 * rank), bf16),
+            pltpu.VMEM((turn, 2 * rank), bf16),
+            pltpu.VMEM((turn, width), bf16),
+            dma((rows,)), dma((rows,)), dma((rows,)), dma((rows,)),
+            dma((2, rows)), dma((2, rows)),
+            dma((6, ctx_size)), dma((6, ctx_size)),
+            dma((devices,)), dma((devices,)),
+            dma((2, ctx_size)), dma((2, ctx_size)),
+            dma((2 * rows + 6,)),
+        ],
+        compiler_params=pltpu.CompilerParams(
+            collective_id=0, has_side_effects=True, vmem_limit_bytes=40 * 1024 * 1024
+        ),
+    )(
+        adapter_owner, shard_lengths, cosine, sine,
+        hidden, q_base, adapter_down[0].T, adapter_up[0],
+        stored_keys, stored_values, unrotated_turn_keys, incoming_values,
+    )
+
+
+def program(mesh):
+    ctx_size, tp_size = mesh.shape["ctx"], mesh.shape["tp"]
+
+    def run(*operands):
+        hidden, q_base, down, keys = operands[0], operands[1], operands[2], operands[7]
+        fits = (
+            ctx_size % 2 == 0
+            and 4 <= ctx_size <= 16
+            and keys.shape[1] == 2 * HEAD_SIZE
+            and q_base.shape[1] % (ctx_size * HEAD_SIZE) == 0
+            and hidden.shape[1] % (tp_size * ctx_size * 128) == 0
+            and hidden.shape[0] % 16 == 0
+            and keys.shape[0] % 16 == 0
+            and 2 * down.shape[2] == 128
+        )
+        if fits:
+            return turn_call(ctx_size, tp_size, *operands)
+        return shards(*operands)
+
+    return run
+
+
 def solution(mesh):
     return jax.shard_map(
-        shards,
+        program(mesh),
         mesh=mesh,
         in_specs=(
             P(("group", "ctx"), None),

time: 146 us -> 66.2 us (0.45)
  blocking collectives: 66 us -> 0 us
  waiting for transfers between devices: 56.8 us -> 0 us
  Pallas kernels: 0 us -> 55.1 us
  between operations: 15 us -> 1.35 us
  local copies, waits for them, and re-layouts: 1.23 us -> 8.79 us
  matrix products: 3.5 us -> 0 us
  other arithmetic: 3.49 us -> 0.43 us
    all_gather x2 -> x0, blocking collectives: 66 us -> none  [the longest x1 34.5 us: shards(): lax.all_gather(key_here, 'ctx', axis=0, tiled=True)]
    psum x1 -> x0, waiting for transfers between devices: 56.8 us -> none  [spread(): return lax.psum(jnp.where(mine, shard, jnp.zeros_like(shard)), axis)]
    pallas_call x0 -> x1, Pallas kernels: none -> 55.1 us  [turn_call(): pl.pallas_call(functools.partial(turn_kernel, ctx_size, tp_size), out_sha...]
    unnamed x19, local copies, waits for them, and re-layouts: 0.8 us -> 8.79 us
    dot_general x3 -> x0, matrix products: 3.5 us -> none  [the longest x1 2.64 us: shards(): adapter_delta = jnp.dot(lowrank, got_up, preferred_element_type=jnp.float32)]
    select_n x4 -> x0, other arithmetic: 2.38 us -> none  [the longest x2 2.29 us: spread(): return lax.psum(jnp.where(mine, shard, jnp.zeros_like(shard)), axis)]
  transfers between devices with their start and end apart: 1 -> 0, of which waited for: 1 -> 0; matrix products, arithmetic and copies ran while one was open for 1% -> 0% of each run, Pallas kernels for 0% -> 0%
where the time goes in v1:
time: 66.2 us; the launch traced here: 65.7 us
  Pallas kernels  55.1 us (83%)
  local copies, waits for them, and re-layouts  8.79 us (13%)
  between operations  1.35 us (2%)
    pallas_call x1, Pallas kernels, turn_call(): pl.pallas_call(functools.partial(turn_kernel, ctx_size, tp_size), out_sha...  55.1 us
    unnamed x19, local copies, waits for them, and re-layouts  8.79 us

profile of v1, /device:TPU:0, one launch (start us, length us, event | category | flops | bytes accessed | tf_op | source)
XLA Modules:
  0.0 65.7 jit_solution(3604311903060452330)
XLA Ops:
  0.7 0.3 fusion
  1.0 0.1 pad_maximum_fusion
  1.8 0.0 copy-start
  1.8 1.6 %copy-done = bf16[1,16384,64]{1,2,0:T(8,128)(2,1)S(1)} copy-done((bf16[1,16384,64]{1,2,0:T(8,128)(2,1)S(1)}, bf16[1,16384,64]{1,2,0:T(8,128)(2,1)}, u32[]{:S(2)}) %copy-start) | copy-done | bytes 2097176
  3.3 0.0 copy-start.1
  3.4 1.0 %copy-done.1 = bf16[16,16384]{1,0:T(8,128)(2,1)S(1)} copy-done((bf16[16,16384]{1,0:T(8,128)(2,1)S(1)}, bf16[16,16384]{1,0:T(8,128)(2,1)}, u32[]{:S(2)}) %copy-start.1) | copy-done | bytes 524312
  4.4 0.0 copy-start.2
  4.4 1.0 %copy-done.2 = bf16[1,64,4096]{2,1,0:T(8,128)(2,1)S(1)} copy-done((bf16[1,64,4096]{2,1,0:T(8,128)(2,1)S(1)}, bf16[1,64,4096]{2,1,0:T(8,128)(2,1)}, u32[]{:S(2)}) %copy-start.2) | copy-done | bytes 524312
  5.4 0.0 copy-start.3
  5.4 0.9 %copy-done.3 = bf16[16,4096]{1,0:T(8,128)(2,1)S(1)} copy-done((bf16[16,4096]{1,0:T(8,128)(2,1)S(1)}, bf16[16,4096]{1,0:T(8,128)(2,1)}, u32[]{:S(2)}) %copy-start.3) | copy-done | bytes 131096
  6.3 0.0 copy-start.4
  6.3 0.8 %copy-done.4 = bf16[64,256]{1,0:T(8,128)(2,1)S(1)} copy-done((bf16[64,256]{1,0:T(8,128)(2,1)S(1)}, bf16[64,256]{1,0:T(8,128)(2,1)}, u32[]{:S(2)}) %copy-start.4) | copy-done | bytes 32792
  7.1 0.0 copy-start.5
  7.1 0.8 %copy-done.5 = bf16[64,256]{1,0:T(8,128)(2,1)S(1)} copy-done((bf16[64,256]{1,0:T(8,128)(2,1)S(1)}, bf16[64,256]{1,0:T(8,128)(2,1)}, u32[]{:S(2)}) %copy-start.5) | copy-done | bytes 32792
  7.9 0.0 copy-start.6
  7.9 0.7 %copy-done.6 = bf16[16,256]{1,0:T(8,128)(2,1)S(1)} copy-done((bf16[16,256]{1,0:T(8,128)(2,1)S(1)}, bf16[16,256]{1,0:T(8,128)(2,1)}, u32[]{:S(2)}) %copy-start.6) | copy-done | bytes 8216
  8.6 0.0 copy-start.7
  8.6 0.7 %copy-done.7 = bf16[16,256]{1,0:T(8,128)(2,1)S(1)} copy-done((bf16[16,256]{1,0:T(8,128)(2,1)S(1)}, bf16[16,256]{1,0:T(8,128)(2,1)}, u32[]{:S(2)}) %copy-start.7) | copy-done | bytes 8216
  9.2 0.0 copy-start.8
  9.3 0.7 copy-done.8
  9.9 55.1 %shard_map.109 = bf16[16,4096]{1,0:T(8,128)(2,1)S(1)} custom-call(s32[1]{0:T(128)S(6)} %copy.13.owner_ref, s32[8]{0:T(128)S(1)} %copy-done.8, f32[128,128]{1,0:T(8,128)S(1)} %get-tuple-element.8.cosine_ref, f32[128,128]{1,0:T(8,128)S(1)} %get-tuple-element.9.sine_ref, bf16[16,16384]{1,0:T(8,128)(2,1)S(1)} %copy-done.1, bf16[16,4096]{1,0:T(8,128)(2,1)S(1)} %copy-done.3, ...), custom_call_target="tpu_custom_call" | custom-call | tf_op jit(solution)/shard_map/pallas_call | solution.py:428
  65.0 0.7 %copy.15 = bf16[16,4096]{1,0:T(8,128)(2,1)} copy(bf16[16,4096]{1,0:T(8,128)(2,1)S(1)} %shard_map.109) | data formatting | bytes 262144
  (2 shorter events, 0.0 us)
Async XLA Ops:
  1.8 1.6 %copy-start = (bf16[1,16384,64]{1,2,0:T(8,128)(2,1)S(1)}, bf16[1,16384,64]{1,2,0:T(8,128)(2,1)}, u32[]{:S(2)}) copy-start(bf16[1,16384,64]{1,2,0:T(8,128)(2,1)} %param.13) | copy-start | bytes 6291460
  3.3 1.0 %copy-start.1 = (bf16[16,16384]{1,0:T(8,128)(2,1)S(1)}, bf16[16,16384]{1,0:T(8,128)(2,1)}, u32[]{:S(2)}) copy-start(bf16[16,16384]{1,0:T(8,128)(2,1)} %hidden_ref.1) | copy-start | bytes 1572868
  4.4 1.0 %copy-start.2 = (bf16[1,64,4096]{2,1,0:T(8,128)(2,1)S(1)}, bf16[1,64,4096]{2,1,0:T(8,128)(2,1)}, u32[]{:S(2)}) copy-start(bf16[1,64,4096]{2,1,0:T(8,128)(2,1)} %param.14) | copy-start | bytes 1572868
  5.4 0.9 %copy-start.3 = (bf16[16,4096]{1,0:T(8,128)(2,1)S(1)}, bf16[16,4096]{1,0:T(8,128)(2,1)}, u32[]{:S(2)}) copy-start(bf16[16,4096]{1,0:T(8,128)(2,1)} %q_ref.1) | copy-start | bytes 393220
  6.3 0.8 %copy-start.4 = (bf16[64,256]{1,0:T(8,128)(2,1)S(1)}, bf16[64,256]{1,0:T(8,128)(2,1)}, u32[]{:S(2)}) copy-start(bf16[64,256]{1,0:T(8,128)(2,1)} %keys_ref.1) | copy-start | bytes 98308
  7.1 0.8 %copy-start.5 = (bf16[64,256]{1,0:T(8,128)(2,1)S(1)}, bf16[64,256]{1,0:T(8,128)(2,1)}, u32[]{:S(2)}) copy-start(bf16[64,256]{1,0:T(8,128)(2,1)} %values_ref.1) | copy-start | bytes 98308
  7.9 0.7 %copy-start.6 = (bf16[16,256]{1,0:T(8,128)(2,1)S(1)}, bf16[16,256]{1,0:T(8,128)(2,1)}, u32[]{:S(2)}) copy-start(bf16[16,256]{1,0:T(8,128)(2,1)} %turn_keys_ref.1) | copy-start | bytes 24580
  8.6 0.7 %copy-start.7 = (bf16[16,256]{1,0:T(8,128)(2,1)S(1)}, bf16[16,256]{1,0:T(8,128)(2,1)}, u32[]{:S(2)}) copy-start(bf16[16,256]{1,0:T(8,128)(2,1)} %turn_values_ref.1) | copy-start | bytes 24580
  9.2 0.7 copy-start.8

commit v2 on v1

--- a/solution.py
+++ b/solution.py
@@ -258,12 +258,6 @@
         ])
     for copies in moved:
         copies[0].start()
-    for copy in up_copies:
-        copy.start()
-    for kind in range(1, 6):
-        for copies in moved:
-            copies[kind].start()
-
     for copy in local:
         copy.wait()
 
@@ -290,7 +284,11 @@
         return sent
 
     down_sent = merge(pair, down_mine, down_pair, down_merged, down_cand, 0)
-    up_sent = merge(up_copies, up_mine, up_pair, up_merged, up_cand, 1)
+    for copy in up_copies:
+        copy.start()
+    for kind in range(1, 6):
+        for copies in moved:
+            copies[kind].start()
     for copies in moved:
         copies[0].wait_recv()
     for copy in down_sent:
@@ -313,6 +311,7 @@
         copy.start()
         summed.append(copy)
     partials[mine_at] = partial[block(me, tokens)]
+    up_sent = merge(up_copies, up_mine, up_pair, up_merged, up_cand, 1)
     for copy in summed:
         copy.wait_recv()
     total = partials[0]
@@ -423,7 +422,7 @@
     sine = jnp.concatenate([-sine, sine], axis=1)
     bf16, f32 = jnp.bfloat16, jnp.float32
     vmem, smem = pl.BlockSpec(memory_space=pltpu.VMEM), pl.BlockSpec(memory_space=pltpu.SMEM)
-    anywhere = pl.BlockSpec(memory_space=pl.ANY)
+    anywhere = pl.BlockSpec(memory_space=pltpu.HBM)
     dma = pltpu.SemaphoreType.DMA
     return pl.pallas_call(
         functools.partial(turn_kernel, ctx_size, tp_size),

time: 66.2 us -> 64.6 us (0.976)
  Pallas kernels: 55.1 us -> 53.6 us
    pallas_call x1, Pallas kernels: 55.1 us -> 53.6 us  [turn_call(): pl.pallas_call(functools.partial(turn_kernel, ctx_size, tp_size), out_sha...]
where the time goes in v2:
time: 64.6 us; the launch traced here: 64.1 us
  Pallas kernels  53.6 us (83%)
  local copies, waits for them, and re-layouts  8.79 us (14%)
  between operations  1.35 us (2%)
    pallas_call x1, Pallas kernels, turn_call(): pl.pallas_call(functools.partial(turn_kernel, ctx_size, tp_size), out_sha...  53.6 us
    unnamed x19, local copies, waits for them, and re-layouts  8.79 us

profile of v2, /device:TPU:0, one launch (start us, length us, event | category | flops | bytes accessed | tf_op | source)
XLA Modules:
  0.0 64.1 jit_solution(171750126727363240)
XLA Ops:
  0.7 0.3 fusion
  1.0 0.1 pad_maximum_fusion
  1.8 0.0 copy-start
  1.8 1.6 %copy-done = bf16[1,16384,64]{1,2,0:T(8,128)(2,1)S(1)} copy-done((bf16[1,16384,64]{1,2,0:T(8,128)(2,1)S(1)}, bf16[1,16384,64]{1,2,0:T(8,128)(2,1)}, u32[]{:S(2)}) %copy-start) | copy-done | bytes 2097176
  3.3 0.0 copy-start.1
  3.4 1.0 %copy-done.1 = bf16[16,16384]{1,0:T(8,128)(2,1)S(1)} copy-done((bf16[16,16384]{1,0:T(8,128)(2,1)S(1)}, bf16[16,16384]{1,0:T(8,128)(2,1)}, u32[]{:S(2)}) %copy-start.1) | copy-done | bytes 524312
  4.4 0.0 copy-start.2
  4.4 1.0 %copy-done.2 = bf16[1,64,4096]{2,1,0:T(8,128)(2,1)S(1)} copy-done((bf16[1,64,4096]{2,1,0:T(8,128)(2,1)S(1)}, bf16[1,64,4096]{2,1,0:T(8,128)(2,1)}, u32[]{:S(2)}) %copy-start.2) | copy-done | bytes 524312
  5.4 0.0 copy-start.3
  5.4 0.9 %copy-done.3 = bf16[16,4096]{1,0:T(8,128)(2,1)S(1)} copy-done((bf16[16,4096]{1,0:T(8,128)(2,1)S(1)}, bf16[16,4096]{1,0:T(8,128)(2,1)}, u32[]{:S(2)}) %copy-start.3) | copy-done | bytes 131096
  6.3 0.0 copy-start.4
  6.3 0.8 %copy-done.4 = bf16[64,256]{1,0:T(8,128)(2,1)S(1)} copy-done((bf16[64,256]{1,0:T(8,128)(2,1)S(1)}, bf16[64,256]{1,0:T(8,128)(2,1)}, u32[]{:S(2)}) %copy-start.4) | copy-done | bytes 32792
  7.1 0.0 copy-start.5
  7.1 0.8 %copy-done.5 = bf16[64,256]{1,0:T(8,128)(2,1)S(1)} copy-done((bf16[64,256]{1,0:T(8,128)(2,1)S(1)}, bf16[64,256]{1,0:T(8,128)(2,1)}, u32[]{:S(2)}) %copy-start.5) | copy-done | bytes 32792
  7.9 0.0 copy-start.6
  7.9 0.7 %copy-done.6 = bf16[16,256]{1,0:T(8,128)(2,1)S(1)} copy-done((bf16[16,256]{1,0:T(8,128)(2,1)S(1)}, bf16[16,256]{1,0:T(8,128)(2,1)}, u32[]{:S(2)}) %copy-start.6) | copy-done | bytes 8216
  8.6 0.0 copy-start.7
  8.6 0.7 %copy-done.7 = bf16[16,256]{1,0:T(8,128)(2,1)S(1)} copy-done((bf16[16,256]{1,0:T(8,128)(2,1)S(1)}, bf16[16,256]{1,0:T(8,128)(2,1)}, u32[]{:S(2)}) %copy-start.7) | copy-done | bytes 8216
  9.2 0.0 copy-start.8
  9.3 0.7 %copy-done.8 = s32[8]{0:T(128)S(1)} copy-done((s32[8]{0:T(128)S(1)}, s32[8]{0:T(128)}, u32[]{:S(2)}) %copy-start.8) | copy-done | bytes 56
  9.9 53.6 %shard_map.109 = bf16[16,4096]{1,0:T(8,128)(2,1)S(1)} custom-call(s32[1]{0:T(128)S(6)} %copy.13.owner_ref, s32[8]{0:T(128)S(1)} %copy-done.8, f32[128,128]{1,0:T(8,128)S(1)} %get-tuple-element.8.cosine_ref, f32[128,128]{1,0:T(8,128)S(1)} %get-tuple-element.9.sine_ref, bf16[16,16384]{1,0:T(8,128)(2,1)S(1)} %copy-done.1, bf16[16,4096]{1,0:T(8,128)(2,1)S(1)} %copy-done.3, ...), custom_call_target="tpu_custom_call" | custom-call | tf_op jit(solution)/shard_map/pallas_call | solution.py:427
  63.5 0.7 %copy.15 = bf16[16,4096]{1,0:T(8,128)(2,1)} copy(bf16[16,4096]{1,0:T(8,128)(2,1)S(1)} %shard_map.109) | data formatting | bytes 262144
  (2 shorter events, 0.0 us)
Async XLA Ops:
  1.8 1.6 %copy-start = (bf16[1,16384,64]{1,2,0:T(8,128)(2,1)S(1)}, bf16[1,16384,64]{1,2,0:T(8,128)(2,1)}, u32[]{:S(2)}) copy-start(bf16[1,16384,64]{1,2,0:T(8,128)(2,1)} %param.13) | copy-start | bytes 6291460
  3.3 1.0 %copy-start.1 = (bf16[16,16384]{1,0:T(8,128)(2,1)S(1)}, bf16[16,16384]{1,0:T(8,128)(2,1)}, u32[]{:S(2)}) copy-start(bf16[16,16384]{1,0:T(8,128)(2,1)} %hidden_ref.1) | copy-start | bytes 1572868
  4.4 1.0 %copy-start.2 = (bf16[1,64,4096]{2,1,0:T(8,128)(2,1)S(1)}, bf16[1,64,4096]{2,1,0:T(8,128)(2,1)}, u32[]{:S(2)}) copy-start(bf16[1,64,4096]{2,1,0:T(8,128)(2,1)} %param.14) | copy-start | bytes 1572868
  5.4 0.9 %copy-start.3 = (bf16[16,4096]{1,0:T(8,128)(2,1)S(1)}, bf16[16,4096]{1,0:T(8,128)(2,1)}, u32[]{:S(2)}) copy-start(bf16[16,4096]{1,0:T(8,128)(2,1)} %q_ref.1) | copy-start | bytes 393220
  6.3 0.8 %copy-start.4 = (bf16[64,256]{1,0:T(8,128)(2,1)S(1)}, bf16[64,256]{1,0:T(8,128)(2,1)}, u32[]{:S(2)}) copy-start(bf16[64,256]{1,0:T(8,128)(2,1)} %keys_ref.1) | copy-start | bytes 98308
  7.1 0.8 %copy-start.5 = (bf16[64,256]{1,0:T(8,128)(2,1)S(1)}, bf16[64,256]{1,0:T(8,128)(2,1)}, u32[]{:S(2)}) copy-start(bf16[64,256]{1,0:T(8,128)(2,1)} %values_ref.1) | copy-start | bytes 98308
  7.9 0.7 %copy-start.6 = (bf16[16,256]{1,0:T(8,128)(2,1)S(1)}, bf16[16,256]{1,0:T(8,128)(2,1)}, u32[]{:S(2)}) copy-start(bf16[16,256]{1,0:T(8,128)(2,1)} %turn_keys_ref.1) | copy-start | bytes 24580
  8.6 0.7 %copy-start.7 = (bf16[16,256]{1,0:T(8,128)(2,1)S(1)}, bf16[16,256]{1,0:T(8,128)(2,1)}, u32[]{:S(2)}) copy-start(bf16[16,256]{1,0:T(8,128)(2,1)} %turn_values_ref.1) | copy-start | bytes 24580
  9.2 0.7 %copy-start.8 = (s32[8]{0:T(128)S(1)}, s32[8]{0:T(128)}, u32[]{:S(2)}) copy-start(s32[8]{0:T(128)} %lengths_ref.1) | copy-start | bytes 100

commit v3 on v2

--- a/solution.py
+++ b/solution.py
@@ -361,6 +361,7 @@
         low_all[:, :rank], up_cand[owner_row], preferred_element_type=jnp.float32
     )
     contract = (((1,), (1,)), ((), ()))
+    sent = []
     for head in range(width // HEAD_SIZE):
         lanes = slice(head * HEAD_SIZE, (head + 1) * HEAD_SIZE)
         query = rotate(
@@ -380,16 +381,17 @@
             old.astype(jnp.bfloat16), old_values, preferred_element_type=jnp.float32
         ) + jnp.dot(new.astype(jnp.bfloat16), new_values, preferred_element_type=jnp.float32)
         attended[:, lanes] = (gathered / denominator).astype(jnp.bfloat16)
-
-    sent = []
-    for far in range(1, ctx_size):
-        to = lax.rem(me + far, ctx_size)
-        copy = remote(
-            attended.at[block(to, tokens)], out_ref.at[:, columns(slot)],
-            late_send.at[1, far], late_recv.at[1, far], to,
-        )
-        copy.start()
-        sent.append(copy)
+        out_lanes = pl.ds(
+            pl.multiple_of(slot * width + head * HEAD_SIZE, HEAD_SIZE), HEAD_SIZE
+        )
+        for far in range(1, ctx_size):
+            to = lax.rem(me + far, ctx_size)
+            copy = remote(
+                attended.at[block(to, tokens), lanes], out_ref.at[:, out_lanes],
+                late_send.at[1 + head, far], late_recv.at[1 + head, far], to,
+            )
+            copy.start()
+            sent.append(copy)
     out_ref[:, columns(slot)] = attended[block(me, tokens)]
     for copy in sent:
         copy.wait_recv()
@@ -447,11 +449,11 @@
             dma((2, rows)), dma((2, rows)),
             dma((6, ctx_size)), dma((6, ctx_size)),
             dma((devices,)), dma((devices,)),
-            dma((2, ctx_size)), dma((2, ctx_size)),
+            dma((1 + width // HEAD_SIZE, ctx_size)), dma((1 + width // HEAD_SIZE, ctx_size)),
             dma((2 * rows + 6,)),
         ],
         compiler_params=pltpu.CompilerParams(
-            collective_id=0, has_side_effects=True, vmem_limit_bytes=40 * 1024 * 1024
+            collective_id=0, has_side_effects=True, vmem_limit_bytes=62 * 1024 * 1024
         ),
     )(
         adapter_owner, shard_lengths, cosine, sine,

time: 64.6 us -> 59.5 us (0.921)
  local copies, waits for them, and re-layouts: 8.79 us -> 1.57 us
  Pallas kernels: 53.6 us -> 55.4 us
    unnamed x19 -> x1, local copies, waits for them, and re-layouts: 8.79 us -> 1.57 us
    pallas_call x1, Pallas kernels: 53.6 us -> 55.4 us  [turn_call(): pl.pallas_call(functools.partial(turn_kernel, ctx_size, tp_size), out_sha...]
where the time goes in v3:
time: 59.5 us; the launch traced here: 59.4 us
  Pallas kernels  55.4 us (93%)
  local copies, waits for them, and re-layouts  1.57 us (3%)
  between operations  1.33 us (2%)
  other arithmetic  1.07 us (2%)
    pallas_call x1, Pallas kernels, turn_call(): pl.pallas_call(functools.partial(turn_kernel, ctx_size, tp_size), out_sha...  55.4 us
    unnamed x1, local copies, waits for them, and re-layouts  1.57 us

profile of v3, /device:TPU:0, one launch (start us, length us, event | category | flops | bytes accessed | tf_op | source)
XLA Modules:
  0.0 59.4 jit_solution(5825026027533020275)
XLA Ops:
  0.7 0.3 fusion
  1.0 0.7 %pad_maximum_fusion = (f32[128,128]{1,0:T(8,128)}, f32[128,128]{1,0:T(8,128)}) fusion(f32[128,64]{1,0:T(8,128)S(1)} %get-tuple-element.7, f32[128,64]{1,0:T(8,128)S(1)} %get-tuple-element.6, f32[128,64]{1,0:T(8,128)S(1)} %get-tuple-element.5), kind=kLoop, calls=%fused_computation.2 | loop fusion | flops 32768 | bytes 229376 | tf_op jit(solution)/shard_map/concatenate | solution.py:423
  2.4 55.4 %shard_map.109 = bf16[16,4096]{1,0:T(8,128)(2,1)} custom-call(s32[1]{0:T(128)S(6)} %copy.13.owner_ref, s32[8]{0:T(128)} %lengths_ref.1, f32[128,128]{1,0:T(8,128)} %get-tuple-element.8.cosine_ref, f32[128,128]{1,0:T(8,128)} %get-tuple-element.9.sine_ref, bf16[16,16384]{1,0:T(8,128)(2,1)} %hidden_ref.1, bf16[16,4096]{1,0:T(8,128)(2,1)} %q_ref.1, ...), custom_call_target="tpu_custom_call" | custom-call | tf_op jit(solution)/shard_map/pallas_call | solution.py:429
  57.8 1.6 %copy.15 = bf16[16,4096]{1,0:T(8,128)(2,1)} copy(bf16[16,4096]{1,0:T(8,128)(2,1)} %shard_map.109) | data formatting | bytes 262144
  (2 shorter events, 0.0 us)

commit v4 on v3

--- a/solution.py
+++ b/solution.py
@@ -239,8 +239,8 @@
             up_ref.at[:, columns((1 - column) * rows + at)], up_pair.at[at],
             up_pair_send.at[far], up_pair_recv.at[far], partner,
         ))
-    for copy in pair:
-        copy.start()
+    for far in (0, 2, 1, 3):
+        pair[far].start()
 
     moved = []
     for far in range(1, ctx_size):
@@ -265,59 +265,80 @@
     owner_row = owner // 2
     is_mine = owner == me
 
-    def merge(copies, mine, other, merged, cand, kind):
+    near = row + 1 - 2 * lax.rem(row, 2)
+    far_row = lax.rem(row + 2, rows)
+    in_row = owner_row == row
+    in_half = owner_row // 2 == row // 2
+
+    def merge_near(copies, mine, other, merged, cand, kind):
         sent = []
-        for far in range(rows):
+        for far in (0, 2, 1, 3):
             at = lax.rem(row + 1 + far, rows)
             copies[far].wait_recv()
-            chosen = lax.select_n(is_mine, other[at], mine[at])
-            if far == rows - 1:
-                cand[row] = chosen
-            else:
-                merged[at] = chosen
+            merged[at] = lax.select_n(is_mine, other[at], mine[at])
+            if far % 2 == 0:
                 copy = remote(
-                    merged.at[at], cand.at[row],
-                    column_send.at[kind, far], column_recv.at[kind, far], at * 2 + column,
+                    merged.at[at], cand.at[at // 2],
+                    column_send.at[kind, at // 2], column_recv.at[kind, at // 2],
+                    near * 2 + column,
                 )
                 copy.start()
                 sent.append(copy)
         return sent
 
-    down_sent = merge(pair, down_mine, down_pair, down_merged, down_cand, 0)
-    for copy in up_copies:
+    def merge_far(sent, merged, cand, kind):
+        for copy in sent:
+            copy.wait_recv()
+        merged[far_row] = lax.select_n(in_row, cand[far_row // 2], merged[far_row])
+        copy = remote(
+            merged.at[far_row], cand.at[2],
+            column_send.at[kind, 2], column_recv.at[kind, 2], far_row * 2 + column,
+        )
         copy.start()
+        cand[3] = lax.select_n(in_row, cand[row // 2], merged[row])
+        return copy
+
+    down_sent = merge_near(pair, down_mine, down_pair, down_merged, down_cand, 0)
+    for far in (0, 2, 1, 3):
+        up_copies[far].start()
     for kind in range(1, 6):
         for copies in moved:
             copies[kind].start()
+    down_last = merge_far(down_sent, down_merged, down_cand, 0)
     for copies in moved:
         copies[0].wait_recv()
-    for copy in down_sent:
-        copy.wait_recv()
+    down_last.wait_recv()
 
     product = lax.dot_general(
-        hid[...], down_cand[owner_row], (((1,), (1,)), ((), ())),
+        hid[...], lax.select_n(in_half, down_cand[2], down_cand[3]), (((1,), (1,)), ((), ())),
         preferred_element_type=jnp.float32,
     )
-    partial[...] = jnp.concatenate([product, jnp.zeros_like(product)], axis=1)
+    split = tokens // 2
+    for index in range(ctx_size):
+        first = index * tokens
+        partial[index * split : (index + 1) * split] = jnp.concatenate(
+            [product[first : first + split], product[first + split : first + tokens]], axis=1
+        )
     summed = []
     mine_at = me * tp_size + core
     for far in range(1, ctx_size * tp_size):
         to = lax.rem(me + far // tp_size, ctx_size)
         copy = remote(
-            partial.at[block(to, tokens)], partials.at[mine_at],
+            partial.at[block(to, split)], partials.at[mine_at],
             part_send.at[far], part_recv.at[far], to,
             lax.rem(core + far % tp_size, tp_size),
         )
         copy.start()
         summed.append(copy)
-    partials[mine_at] = partial[block(me, tokens)]
-    up_sent = merge(up_copies, up_mine, up_pair, up_merged, up_cand, 1)
+    partials[mine_at] = partial[block(me, split)]
+    up_sent = merge_near(up_copies, up_mine, up_pair, up_merged, up_cand, 1)
     for copy in summed:
         copy.wait_recv()
     total = partials[0]
     for number in range(1, ctx_size * tp_size):
         total = total + partials[number]
-    lowrank = total.astype(jnp.bfloat16)
+    lowrank = jnp.concatenate([total[:, :rank], total[:, rank:]], axis=0)
+    lowrank = jnp.concatenate([lowrank, lowrank], axis=1).astype(jnp.bfloat16)
     low_mine[...] = lowrank
     low_all[block(me, tokens)] = lowrank
     low_sent = []
@@ -329,11 +350,10 @@
         copy.start()
         low_sent.append(copy)
 
+    up_last = merge_far(up_sent, up_merged, up_cand, 1)
     for kind in range(1, 6):
         for copies in moved:
             copies[kind].wait_recv()
-    for copy in up_sent:
-        copy.wait_recv()
     cosine = cosine_ref[...]
     sine = sine_ref[...]
 
@@ -357,8 +377,9 @@
 
     for copy in low_sent:
         copy.wait_recv()
+    up_last.wait_recv()
     delta = jnp.dot(
-        low_all[:, :rank], up_cand[owner_row], preferred_element_type=jnp.float32
+        low_all[:, :rank], lax.select_n(in_half, up_cand[2], up_cand[3]), preferred_element_type=jnp.float32
     )
     contract = (((1,), (1,)), ((), ()))
     sent = []
@@ -395,7 +416,7 @@
     out_ref[:, columns(slot)] = attended[block(me, tokens)]
     for copy in sent:
         copy.wait_recv()
-    for copies in [pair, up_copies, down_sent, up_sent, summed, low_sent, sent] + moved:
+    for copies in [pair, up_copies, down_sent, up_sent, [down_last, up_last], summed, low_sent, sent] + moved:
         for copy in copies:
             copy.wait_send()
 
@@ -440,8 +461,8 @@
             pltpu.VMEM((slots * ctx_size, HEAD_SIZE), bf16),
             pltpu.VMEM((turn, HEAD_SIZE), bf16),
             pltpu.VMEM((turn, HEAD_SIZE), bf16),
-            pltpu.VMEM((turn, 2 * rank), f32),
-            pltpu.VMEM((devices, tokens, 2 * rank), f32),
+            pltpu.VMEM((turn // 2, 2 * rank), f32),
+            pltpu.VMEM((devices, tokens // 2, 2 * rank), f32),
             pltpu.VMEM((tokens, 2 * rank), bf16),
             pltpu.VMEM((turn, 2 * rank), bf16),
             pltpu.VMEM((turn, width), bf16),
@@ -469,7 +490,7 @@
         hidden, q_base, down, keys = operands[0], operands[1], operands[2], operands[7]
         fits = (
             ctx_size % 2 == 0
-            and 4 <= ctx_size <= 16
+            and ctx_size == 8
             and keys.shape[1] == 2 * HEAD_SIZE
             and q_base.shape[1] % (ctx_size * HEAD_SIZE) == 0
             and hidden.shape[1] % (tp_size * ctx_size * 128) == 0

time: 59.5 us -> 63.4 us (1.066)
  Pallas kernels: 55.4 us -> 59.3 us
    pallas_call x1, Pallas kernels: 55.4 us -> 59.3 us  [turn_call(): pl.pallas_call(functools.partial(turn_kernel, ctx_size, tp_size), out_sha...]
where the time goes in v4:
time: 63.4 us; the launch traced here: 63.2 us
  Pallas kernels  59.3 us (94%)
  local copies, waits for them, and re-layouts  1.57 us (2%)
  between operations  1.33 us (2%)
  other arithmetic  1.07 us (2%)
    pallas_call x1, Pallas kernels, turn_call(): pl.pallas_call(functools.partial(turn_kernel, ctx_size, tp_size), out_sha...  59.3 us
    unnamed x1, local copies, waits for them, and re-layouts  1.57 us

profile of v4, /device:TPU:0, one launch (start us, length us, event | category | flops | bytes accessed | tf_op | source)
XLA Modules:
  0.0 63.2 jit_solution(3894039734452123496)
XLA Ops:
  0.7 0.3 fusion
  1.0 0.7 %pad_maximum_fusion = (f32[128,128]{1,0:T(8,128)}, f32[128,128]{1,0:T(8,128)}) fusion(f32[128,64]{1,0:T(8,128)S(1)} %get-tuple-element.7, f32[128,64]{1,0:T(8,128)S(1)} %get-tuple-element.6, f32[128,64]{1,0:T(8,128)S(1)} %get-tuple-element.5), kind=kLoop, calls=%fused_computation.2 | loop fusion | flops 32768 | bytes 229376 | tf_op jit(solution)/shard_map/concatenate | solution.py:444
  2.4 59.3 %shard_map.109 = bf16[16,4096]{1,0:T(8,128)(2,1)} custom-call(s32[1]{0:T(128)S(6)} %copy.13.owner_ref, s32[8]{0:T(128)} %lengths_ref.1, f32[128,128]{1,0:T(8,128)} %get-tuple-element.8.cosine_ref, f32[128,128]{1,0:T(8,128)} %get-tuple-element.9.sine_ref, bf16[16,16384]{1,0:T(8,128)(2,1)} %hidden_ref.1, bf16[16,4096]{1,0:T(8,128)(2,1)} %q_ref.1, ...), custom_call_target="tpu_custom_call" | custom-call | tf_op jit(solution)/shard_map/pallas_call | solution.py:450
  61.7 1.6 %copy.15 = bf16[16,4096]{1,0:T(8,128)(2,1)} copy(bf16[16,4096]{1,0:T(8,128)(2,1)} %shard_map.109) | data formatting | bytes 262144
  (2 shorter events, 0.0 us)
